TPU v7x, 32 devices: a whole 2x2x4 slice. The times are simulated.
32 devices in a mesh: groups: 2 (over y), attn: 4 (over z), expert: 4 (over x, core).
Axes of the slice: x: 2, y: 2, z: 4, core: 2. Of those that a mesh axis runs over, the one named last changes fastest.
Arguments:
- hidden_in: bfloat16 [512, 6144], P(('groups', 'attn')), parts along dimension 0, may hold values from -6 to 6
- queries: bfloat16 [512, 6144], P(('groups', 'attn'), 'expert'), parts along dimension 0, may hold values from -5 to 5
- keys: bfloat16 [512, 1024], P(('groups', 'attn'), 'expert'), parts along dimension 0, may hold values from -5 to 5
- values: bfloat16 [512, 1024], P(('groups', 'attn'), 'expert'), parts along dimension 0, may hold values from -6 to 6
- norm_gain: bfloat16 [6144], replicated, may hold values from 0.099609375 to 1.8984375
- routes: int32 [512, 2], P(('groups', 'attn')), parts along dimension 0, may hold values from 0 to 3, all different within a row; in each aligned block of 64 rows (0 to 63, 64 to 127, ...) at most 48 rows name the same one
- gate_codes: int32 [512, 2], P(('groups', 'attn')), parts along dimension 0, may hold values from 1 to 255
- lengths: int32 [8], P('groups'), parts along dimension 0, may hold values from 1 to 128, 256 in all
- w_gate: bfloat16 [4, 6144, 8192], P('expert', None, 'attn'), may hold values from -0.078125 to 0.078125
- w_up: bfloat16 [4, 6144, 8192], P('expert', None, 'attn'), may hold values from -0.078125 to 0.078125
- w_down: bfloat16 [4, 8192, 6144], P('expert', 'attn'), may hold values from -0.0625 to 0.0625
Outputs:
- mixed: bfloat16 [512, 6144], P(('groups', 'attn'), 'expert'), parts along dimension 0
There are 2 independent parts, one for each index of `groups`. A program takes and returns all parts, laid end to end along the dimension named above; an argument that names none is the same for every part. Nothing has to cross between parts.
Inputs may be any that keep to these rules, and one draw needn't show every extreme that they name: `routes`: each row names two different experts; of the 64 tokens of one index of attn (aligned blocks of rows) at most 48 name any one expert, a bound that some block reaches of them. `lengths`: they sum to 256, and the longest has exactly 128 tokens.
All inputs are finite; a program needn't handle non-finite values.
Results may differ from a plain program's by a relative error of at most 0.008.
Values may be sent and summed in bfloat16 or wider, within the bound.
A program may use at most 192 MiB of HBM per device.

v0:
```python
import math

import jax
import jax.numpy as jnp
from jax import lax
from jax.sharding import PartitionSpec as P

QH = 48
KVH = 8
HD = 128


NEG_FILL = -1e30


def local(
    hidden_in, queries, keys, values, norm_gain, routes, gate_codes, lengths, w_gate, w_up, w_down
):
    tok_rows = queries.shape[0]
    per_group = QH // KVH
    kv_local = keys.shape[1] // HD
    whole_keys, whole_values = (
        lax.all_gather(keys, "attn", axis=0, tiled=True),
        lax.all_gather(values, "attn", axis=0, tiled=True),
    )
    all_rows_count = whole_keys.shape[0]
    first_row = lax.axis_index("attn") * tok_rows
    query_pos = first_row + jnp.arange(tok_rows, dtype=jnp.int32)
    key_pos = jnp.arange(all_rows_count, dtype=jnp.int32)
    bounds = jnp.cumsum(lengths)
    query_doc = jnp.sum((query_pos[:, None] >= bounds[None, :]).astype(jnp.int32), axis=1)
    key_doc = jnp.sum((key_pos[:, None] >= bounds[None, :]).astype(jnp.int32), axis=1)
    allowed = (query_doc[:, None] == key_doc[None, :]) & (key_pos[None, :] <= query_pos[:, None])
    query_heads = queries.reshape(tok_rows, kv_local, per_group, HD)
    key_heads = whole_keys.reshape(all_rows_count, kv_local, HD)
    value_heads = whole_values.reshape(all_rows_count, kv_local, HD)
    scores = jnp.einsum(
        "qhgd,khd->hgqk", query_heads, key_heads, preferred_element_type=jnp.float32
    ) * (1.0 / math.sqrt(HD))
    scores = jnp.where(allowed[None, None], scores, NEG_FILL)
    row_top = jnp.max(scores, axis=3, keepdims=True)
    weights = jnp.where(allowed[None, None], jnp.exp(scores - row_top), jnp.float32(0.0))
    totals = jnp.sum(weights, axis=3)
    numerator = jnp.einsum(
        "hgqk,khd->qhgd",
        weights.astype(jnp.bfloat16),
        value_heads,
        preferred_element_type=jnp.float32,
    )
    attended = (numerator / jnp.transpose(totals, (2, 0, 1))[:, :, :, None]).astype(jnp.bfloat16)
    attended = attended.reshape(tok_rows, kv_local * per_group * HD)
    full_heads = lax.all_gather(attended, "expert", axis=1, tiled=True)
    residual = hidden_in.astype(jnp.float32) + full_heads.astype(jnp.float32)
    scale_row = lax.rsqrt(jnp.mean(residual * residual, axis=1, keepdims=True) + 1e-05)
    normed = (residual * scale_row * norm_gain.astype(jnp.float32)[None, :]).astype(jnp.bfloat16)
    codes = gate_codes.astype(jnp.float32)
    gate_share = codes / jnp.sum(codes, axis=1, keepdims=True)
    expert_base = lax.axis_index("expert") * w_gate.shape[0]
    route_hits = routes == expert_base + 0
    chosen = jnp.any(route_hits, axis=1)
    route_weight = jnp.sum(jnp.where(route_hits, gate_share, jnp.float32(0.0)), axis=1)
    gate_w = w_gate[0]
    up_w = w_up[0]
    down_w = w_down[0]
    masked = jnp.where(chosen[:, None], normed, jnp.zeros_like(normed))
    block_rows = lax.all_gather(masked, "attn", axis=0, tiled=True)
    gate = jnp.dot(block_rows, gate_w, preferred_element_type=jnp.float32)
    up_val = jnp.dot(block_rows, up_w, preferred_element_type=jnp.float32)
    activated = (jax.nn.silu(gate) * up_val).astype(jnp.bfloat16)
    routed = lax.psum_scatter(
        jnp.dot(activated, down_w, preferred_element_type=jnp.float32).astype(jnp.bfloat16),
        "attn",
        scatter_dimension=0,
        tiled=True,
    ).astype(jnp.float32)
    combined = route_weight[:, None] * routed
    col_width = combined.shape[1] // lax.axis_size("expert")
    col_start = lax.axis_index("expert") * col_width
    full_sum = lax.psum(combined.astype(jnp.bfloat16), "expert").astype(jnp.float32)
    own_share = lax.dynamic_slice_in_dim(full_sum, col_start, col_width, 1)
    own_resid = lax.dynamic_slice_in_dim(residual, col_start, col_width, 1)
    return (own_resid + own_share).astype(jnp.bfloat16)


def solution(mesh):
    placed = (
        P(("groups", "attn"), None),
        P(("groups", "attn"), "expert"),
        P(("groups", "attn"), "expert"),
        P(("groups", "attn"), "expert"),
        P(),
        P(("groups", "attn"), None),
        P(("groups", "attn"), None),
        P("groups"),
        P("expert", None, "attn"),
        P("expert", None, "attn"),
        P("expert", "attn", None),
    )
    return jax.shard_map(
        local,
        mesh=mesh,
        in_specs=placed,
        out_specs=P(("groups", "attn"), "expert"),
        check_vma=False,
    )
```

profile of v0, /device:TPU:0, one launch (start us, length us, event | category | flops | bytes accessed | tf_op | source)
XLA Modules:
  0.0 255.1 jit_solution(17923414568325104464)
XLA Ops:
  6.5 0.8 reduce-window.8
  7.4 0.1 convert_reduce_fusion
  7.5 0.1 convert_reduce_fusion.1
  7.5 15.3 %all_gather.12 = bf16[256,256]{1,0:T(8,128)(2,1)S(1)} all-gather(bf16[64,256]{1,0:T(8,128)(2,1)} %param.13), channel_id=1, replica_groups=mesh['groups'=2,'attn'=4,'expert'=4] {'attn'}, dimensions={0}, use_global_device_ids=true | all-gather | bytes 163840 | tf_op jit(solution)/shard_map/all_gather | solution.py:23
  22.8 0.1 copy.25
  22.9 1.2 reshape.104
  24.1 0.1 fusion.34
  24.2 0.3 fusion.27
  24.4 0.5 fusion.44
  24.9 13.5 %all_gather.13 = bf16[256,256]{1,0:T(8,128)(2,1)S(1)} all-gather(bf16[64,256]{1,0:T(8,128)(2,1)S(1)} %copy-done.1), channel_id=1, replica_groups=mesh['groups'=2,'attn'=4,'expert'=4] {'attn'}, dimensions={0}, use_global_device_ids=true | all-gather | bytes 163840 | tf_op jit(solution)/shard_map/all_gather | solution.py:24
  38.4 0.1 copy.28
  38.6 0.3 fusion.29
  38.9 0.1 copy.30
  39.0 0.2 reshape.106
  39.3 0.0 copy-start.2
  39.3 0.0 copy-start.3
  39.3 8.6 %all_gather.14 = bf16[64,6144]{1,0:T(8,128)(2,1)S(1)} all-gather(bf16[64,1536]{1,0:T(8,128)(2,1)S(1)} %reshape.106), channel_id=1, replica_groups=mesh['groups'=2,'attn'=4,'expert'=4] {'expert'}, dimensions={1}, use_global_device_ids=true | all-gather | bytes 983040 | tf_op jit(solution)/shard_map/all_gather | solution.py:52
  47.9 0.4 multiply_reduce_fusion
  48.3 1.2 fusion.31
  49.6 0.0 all-gather.2.cloned.1.call-update
  49.6 0.0 reduce-scatter.2.cloned.1.call-start
  49.6 63.9 %all-gather.2.cloned.1.call-done = bf16[256,6144]{1,0:T(8,128)(2,1)} async-done(((bf16[64,6144]{1,0:T(8,128)(2,1)}), bf16[256,6144]{1,0:T(8,128)(2,1)}) %all-gather.2.cloned.1.call-update) | async-done | bytes 3145744 | tf_op jit(solution)/shard_map/all_gather | solution.py:66
  113.6 13.4 %fusion.5 = f32[256,2048]{1,0:T(8,128)} fusion(bf16[256,6144]{1,0:T(8,128)(2,1)} %all-gather.2.cloned.1.call-done, bf16[1,6144,2048]{2,1,0:T(8,128)(2,1)} %param.19), kind=kOutput, calls=%fused_computation.5 | convolution fusion | flops 6442450944 | bytes 30408704 | tf_op jit(solution)/shard_map/dot_general | solution.py:67
  127.0 23.8 %fusion.7 = bf16[256,6144]{1,0:T(8,128)(2,1)} fusion(bf16[1,2048,6144]{2,1,0:T(8,128)(2,1)} %param.21, bf16[256,6144]{1,0:T(8,128)(2,1)} %all-gather.2.cloned.1.call-done, bf16[1,6144,2048]{2,1,0:T(8,128)(2,1)} %param.20, f32[256,2048]{1,0:T(8,128)} %fusion.5), kind=kOutput, calls=%fused_computation.7 | convolution fusion | flops 12889620480 | bytes 58720256 | tf_op jit(solution)/shard_map/dot_general | solution.py:71
  150.8 0.0 reduce-scatter.2.cloned.1.call-update
  150.8 0.0 all-reduce.2.cloned.1.call-start
  150.8 0.6 copy-done.4
  151.5 58.4 %reduce-scatter.2.cloned.1.call-done = bf16[64,6144]{1,0:T(8,128)(2,1)} async-done(((bf16[256,6144]{1,0:T(8,128)(2,1)}), bf16[64,6144]{1,0:T(8,128)(2,1)}) %reduce-scatter.2.cloned.1.call-update) | async-done | bytes 786448 | tf_op jit(solution)/shard_map/reduce_scatter | solution.py:70
  209.9 2.2 multiply_convert_fusion
  212.1 0.0 all-reduce.2.cloned.1.call-update
  212.1 34.8 %all-reduce.2.cloned.1.call-done = bf16[64,6144]{1,0:T(8,128)(2,1)} async-done(((bf16[64,6144]{1,0:T(8,128)(2,1)}), bf16[64,6144]{1,0:T(8,128)(2,1)}) %all-reduce.2.cloned.1.call-update) | async-done | bytes 786448 | tf_op jit(solution)/shard_map/psum | solution.py:79
  246.9 1.6 add_convert_fusion
  (14 shorter events, 0.1 us)
Async XLA Ops:
  6.5 18.4 %copy-start.1 = (bf16[64,256]{1,0:T(8,128)(2,1)S(1)}, bf16[64,256]{1,0:T(8,128)(2,1)}, u32[]{:S(2)}) copy-start(bf16[64,256]{1,0:T(8,128)(2,1)} %param.14) | copy-start | bytes 98308
  6.5 107.0 %all-gather.2.cloned.1.call-start = ((), (), s32[]{:S(2)}) async-start(), calls=%async_computation.1 | async-start | bytes 3932160 | tf_op jit(solution)/shard_map/all_gather | solution.py:66
  38.5 9.4 %copy-start = (bf16[64,6144]{1,0:T(8,128)(2,1)S(1)}, bf16[64,6144]{1,0:T(8,128)(2,1)}, u32[]{:S(2)}) copy-start(bf16[64,6144]{1,0:T(8,128)(2,1)} %param.11) | copy-start | bytes 2359300
  39.3 9.0 %copy-start.2 = (bf16[6144]{0:T(1024)(128)(2,1)S(1)}, bf16[6144]{0:T(1024)(128)(2,1)}, u32[]{:S(2)}) copy-start(bf16[6144]{0:T(1024)(128)(2,1)} %param.15) | copy-start | bytes 36868
  39.3 9.0 %copy-start.3 = (s32[64,2]{0,1:T(2,128)S(1)}, s32[64,2]{0,1:T(2,128)}, u32[]{:S(2)}) copy-start(s32[64,2]{0,1:T(2,128)} %param.16) | copy-start | bytes 1540
  49.6 160.3 %reduce-scatter.2.cloned.1.call-start = ((), (), s32[]{:S(2)}) async-start(), calls=%async_computation.2 | async-start | bytes 3932160 | tf_op jit(solution)/shard_map/reduce_scatter | solution.py:70
  150.8 0.7 copy-start.4
  150.8 96.1 %all-reduce.2.cloned.1.call-start = ((), (), s32[]{:S(2)}) async-start(), calls=%async_computation.3 | async-start | bytes 1572864 | tf_op jit(solution)/shard_map/psum | solution.py:79
Sparse Core Ops, SparseCore 0:
  49.7 63.8 all-gather.1
  150.9 58.8 reduce-scatter.1
  212.2 34.6 all-reduce.1
where the time goes:
time: 255 us
  waiting for transfers between devices  157 us (62%)
  matrix products  38.2 us (15%)
  blocking collectives  37.4 us (15%)
  between operations  13.2 us (5%)
  other arithmetic  6.62 us (3%)
    all_gather x1, waiting for transfers between devices, local(): block_rows = lax.all_gather(masked, 'attn', axis=0, tiled=True)  63.9 us
    reduce_scatter x1, waiting for transfers between devices, local(): lax.psum_scatter(jnp.dot(activated, down_w, preferred_element_type=jnp.fl...  58.4 us
    psum x1, waiting for transfers between devices, local(): lax.psum(combined.astype(jnp.bfloat16), 'expert').astype(jnp.float32)  34.8 us
    dot_general x1, matrix products, local(): jnp.dot(activated, down_w, preferred_element_type=jnp.float32)  23.8 us
    all_gather x1, blocking collectives, local(): lax.all_gather(keys, 'attn', axis=0, tiled=True)  15.3 us
    all_gather x1, blocking collectives, local(): lax.all_gather(values, 'attn', axis=0, tiled=True)  13.5 us
    dot_general x1, matrix products, local(): gate = jnp.dot(block_rows, gate_w, preferred_element_type=jnp.float32)  13.4 us
    all_gather x1, blocking collectives, local(): full_heads = lax.all_gather(attended, 'expert', axis=1, tiled=True)  8.6 us
  transfers between devices with their start and end apart: 3, of which 3 were waited for; matrix products, arithmetic and copies ran while one was open for 0% of the time, Pallas kernels for 0%

commit v1 on v0

--- a/solution.py
+++ b/solution.py
@@ -1,8 +1,11 @@
+import functools
 import math
 
 import jax
 import jax.numpy as jnp
 from jax import lax
+from jax.experimental import pallas as pl
+from jax.experimental.pallas import tpu as pltpu
 from jax.sharding import PartitionSpec as P
 
 QH = 48
@@ -82,6 +85,343 @@
     return (own_resid + own_share).astype(jnp.bfloat16)
 
 
+MESH = pl.DeviceIdType.MESH
+SLOTS = 14
+CW = 256
+
+
+def remote(src, dst, send, recv, dev):
+    return pltpu.make_async_remote_copy(
+        src_ref=src, dst_ref=dst, send_sem=send, recv_sem=recv, device_id=dev, device_id_type=MESH
+    )
+
+
+def fused_kernel(
+    nz, q_ref, k_ref, v_ref, gain_ref, routes_ref, codes_ref, len_ref, hid_hbm, wg_hbm, wu_hbm, wd_hbm,
+    out_ref,
+    wbuf, kall, vall, hid, res, gall, meta, ssq, act, part, rcore, rx, rz,
+    wsem, hsem, kv_s, kv_r, q_s, q_r, m_s, m_r, gz_s, gz_r, gx_s, gx_r, gc_s, gc_r,
+    pc_s, pc_r, px_s, px_r, pz_s, pz_r,
+):
+    y = lax.axis_index("groups")
+    z = lax.axis_index("attn")
+    e = lax.axis_index("expert")
+    xx, cc = e // 2, e % 2
+    tok, width = q_ref.shape
+    rows = nz * tok
+    ffl = act.shape[1]
+    n_pair = ffl // CW
+    n_chunks = 3 * n_pair
+    per_slice = n_pair // 4
+    three = wbuf.shape[1] // ffl
+    ex, ec, ed = (1 - xx) * 2 + cc, xx * 2 + 1 - cc, (1 - xx) * 2 + 1 - cc
+    to_x, to_c = (y, z, ex), (y, z, ec)
+    order = [ed, ec, ex, e]
+
+    def rowsof(zi):
+        return pl.ds(pl.multiple_of(zi * tok, tok), tok)
+
+    def up_to(d):
+        return lax.rem(z + d, nz)
+
+    def down_to(d):
+        return lax.rem(z + nz - d, nz)
+
+    def gate_copy(j, slot):
+        return pltpu.make_async_copy(
+            wg_hbm.at[0, :, pl.ds(pl.multiple_of(j * CW, CW), CW)], wbuf.at[slot], wsem.at[slot, 0]
+        )
+
+    def up_copy(j, slot):
+        return pltpu.make_async_copy(
+            wu_hbm.at[0, :, pl.ds(pl.multiple_of(j * CW, CW), CW)], wbuf.at[slot], wsem.at[slot, 0]
+        )
+
+    def down_copies(k, slot):
+        pos = k // per_slice
+        ep = jnp.where(pos == 0, ed, jnp.where(pos == 1, ec, jnp.where(pos == 2, ex, e)))
+        base = ep * width + (k % per_slice) * (three * CW)
+        return [
+            pltpu.make_async_copy(
+                wd_hbm.at[0, :, pl.ds(pl.multiple_of(base + t * CW, CW), CW)],
+                wbuf.at[slot, pl.ds(t * ffl, ffl)],
+                wsem.at[slot, t],
+            )
+            for t in range(three)
+        ]
+
+    hcopy = pltpu.make_async_copy(
+        hid_hbm.at[:, pl.ds(pl.multiple_of(e * width, width), width)], hid, hsem
+    )
+    hcopy.start()
+
+    @pl.loop(0, SLOTS // 2)
+    def _(j):
+        gate_copy(j, 2 * j).start()
+        up_copy(j, 2 * j + 1).start()
+
+    barrier = pltpu.get_barrier_semaphore()
+    peers = [(y, up_to(d), e) for d in range(1, nz)] + [(y, z, ex), (y, z, ec), (y, z, ed)]
+    for dev in peers:
+        pl.semaphore_signal(barrier, inc=1, device_id=dev, device_id_type=MESH)
+    pl.semaphore_wait(barrier, len(peers))
+
+    kv = []
+    for d in range(1, nz):
+        dev = (y, up_to(d), e)
+        for i, (a, b) in enumerate(((k_ref, kall), (v_ref, vall))):
+            cp = remote(a, b.at[rowsof(z)], kv_s.at[i, d], kv_r.at[i, d], dev)
+            cp.start()
+            kv.append(cp)
+    kall[rowsof(z), :] = k_ref[...]
+    vall[rowsof(z), :] = v_ref[...]
+
+    lane = lax.broadcasted_iota(jnp.int32, (tok, 128), 1)
+    codes = codes_ref[...].astype(jnp.float32)
+    share = codes / (codes[:, 0:1] + codes[:, 1:2])
+    routes = routes_ref[...]
+    wts = jnp.where(routes[:, 0:1] == lane, share[:, 0:1], 0.0) + jnp.where(
+        routes[:, 1:2] == lane, share[:, 1:2], 0.0
+    )
+
+    qpos = z * tok + lax.broadcasted_iota(jnp.int32, (tok, rows), 0)
+    kpos = lax.broadcasted_iota(jnp.int32, (tok, rows), 1)
+    qdoc = jnp.zeros((tok, rows), jnp.int32)
+    kdoc = jnp.zeros((tok, rows), jnp.int32)
+    bound = jnp.int32(0)
+    for s in range(len_ref.shape[0]):
+        bound = bound + len_ref[s]
+        qdoc = qdoc + (qpos >= bound).astype(jnp.int32)
+        kdoc = kdoc + (kpos >= bound).astype(jnp.int32)
+    allowed = (qdoc == kdoc) & (kpos <= qpos)
+
+    for cp in kv:
+        cp.wait_recv()
+    hcopy.wait()
+
+    per_group = QH // KVH
+    total = jnp.zeros((tok, 1), jnp.float32)
+    for h in range(width // HD):
+        g = h // per_group
+        cols = slice(h * HD, (h + 1) * HD)
+        gcols = slice(g * HD, (g + 1) * HD)
+        sc = lax.dot_general(
+            q_ref[:, cols], kall[:, gcols], (((1,), (1,)), ((), ())),
+            preferred_element_type=jnp.float32,
+        ) * (1.0 / math.sqrt(HD))
+        sc = jnp.where(allowed, sc, NEG_FILL)
+        top = jnp.max(sc, axis=1, keepdims=True)
+        w = jnp.where(allowed, jnp.exp(sc - top), 0.0)
+        tot = jnp.sum(w, axis=1, keepdims=True)
+        num = jnp.dot(w.astype(jnp.bfloat16), vall[:, gcols], preferred_element_type=jnp.float32)
+        att = (num / tot).astype(jnp.bfloat16)
+        r = hid[:, cols].astype(jnp.float32) + att.astype(jnp.float32)
+        res[:, cols] = r
+        total = total + jnp.sum(r * r, axis=1, keepdims=True)
+        gn = gain_ref[:, pl.ds(pl.multiple_of(e * width + h * HD, HD), HD)].astype(jnp.float32)
+        gall[e, rowsof(z), cols] = (r * gn).astype(jnp.bfloat16)
+
+    own = gall.at[e, rowsof(z)]
+    sends = []
+    gz = []
+    ssq[0] = jnp.broadcast_to(total, (tok, 128))
+    qc = []
+    for i, pe in enumerate((ex, ec, ed)):
+        cp = remote(ssq.at[0], ssq.at[i + 1], q_s.at[i], q_r.at[i], (y, z, pe))
+        cp.start()
+        qc.append(cp)
+    for d in range(1, nz):
+        cp = remote(own, own, gz_s.at[d], gz_r.at[d], (y, up_to(d), e))
+        cp.start()
+        gz.append(cp)
+
+    def forward(zi, d):
+        blk = gall.at[e, rowsof(zi)]
+        a = remote(blk, blk, gx_s.at[d], gx_r.at[d], to_x)
+        a.start()
+        b = remote(blk, blk, gc_s.at[0, d], gc_r.at[0, d], to_c)
+        b.start()
+        sends.extend([a, b])
+
+    forward(z, 0)
+    for cp in qc:
+        cp.wait_recv()
+    ms = ssq[0] + ssq[1] + ssq[2] + ssq[3]
+    scale = lax.rsqrt(ms * (1.0 / (4 * width)) + 1e-05)
+    meta[rowsof(z), :] = jnp.where(lane == 4, scale, wts)
+    mc = []
+    for d in range(1, nz):
+        blk = meta.at[rowsof(z)]
+        cp = remote(blk, blk, m_s.at[d], m_r.at[d], (y, up_to(d), e))
+        cp.start()
+        mc.append(cp)
+    for d in range(1, nz):
+        gz[d - 1].wait_recv()
+        forward(down_to(d), d)
+    for d in range(nz):
+        zi = down_to(d)
+        blk = gall.at[ex, rowsof(zi)]
+        remote(blk, blk, gx_s.at[d], gx_r.at[d], to_x).wait_recv()
+        b = remote(blk, blk, gc_s.at[1, d], gc_r.at[1, d], to_c)
+        b.start()
+        sends.append(b)
+    for cp in mc:
+        cp.wait_recv()
+    for d in range(nz):
+        zi = down_to(d)
+        for i, pe in enumerate((ec, ed)):
+            blk = gall.at[pe, rowsof(zi)]
+            remote(blk, blk, gc_s.at[i, d], gc_r.at[i, d], to_c).wait_recv()
+
+    scol = meta[:, 4:5]
+    mlane = lax.broadcasted_iota(jnp.int32, (rows, 128), 1)
+    wcol = jnp.sum(jnp.where(mlane == e, meta[...], 0.0), axis=1, keepdims=True)
+
+    def big(slot):
+        acc = jnp.zeros((rows, CW), jnp.float32)
+        for i in range(4):
+            acc = acc + jnp.dot(
+                gall[i], wbuf[slot, i * width : (i + 1) * width, :],
+                preferred_element_type=jnp.float32,
+            )
+        return acc
+
+    @pl.loop(0, n_pair)
+    def _(j):
+        sg = lax.rem(2 * j, SLOTS)
+        su = lax.rem(2 * j + 1, SLOTS)
+        gate_copy(j, sg).wait()
+        gate = big(sg) * scol
+        up_copy(j, su).wait()
+        upv = big(su) * scol
+        hv = (gate / (1.0 + jnp.exp(-gate))) * upv
+        act[:, pl.ds(pl.multiple_of(j * CW, CW), CW)] = hv.astype(jnp.bfloat16)
+        nxt = 2 * j + SLOTS
+
+        @pl.when(nxt < 2 * n_pair)
+        def _():
+            gate_copy(nxt // 2, sg).start()
+            up_copy(nxt // 2, su).start()
+
+        @pl.when((nxt >= 2 * n_pair) & (nxt < n_chunks))
+        def _():
+            for cp in down_copies(nxt - 2 * n_pair, sg) + down_copies(nxt + 1 - 2 * n_pair, su):
+                cp.start()
+
+    def down_slice(pos):
+        @pl.loop(0, per_slice)
+        def _(i):
+            k = pos * per_slice + i
+            slot = lax.rem(2 * n_pair + k, SLOTS)
+            for t, cp in enumerate(down_copies(k, slot)):
+                cp.wait()
+                o = jnp.dot(
+                    act[...], wbuf[slot, t * ffl : (t + 1) * ffl, :],
+                    preferred_element_type=jnp.float32,
+                )
+                col = pl.ds(pl.multiple_of((i * three + t) * CW, CW), CW)
+                part[pos, :, col] = (o * wcol).astype(jnp.bfloat16)
+
+    pc = []
+    for pos in range(2):
+        down_slice(pos)
+        cp = remote(part.at[pos], rcore.at[pos], pc_s.at[pos], pc_r.at[pos], to_c)
+        cp.start()
+        pc.append(cp)
+    down_slice(2)
+    pc[0].wait_recv()
+    steps = [2, 1, 3, 0] if nz == 4 else list(range(1, nz)) + [0]
+    px = []
+    for n, d in enumerate(steps):
+        rr = rowsof(up_to(d))
+        part[2, rr, :] = (
+            part[2, rr, :].astype(jnp.float32) + rcore[0, rr, :].astype(jnp.float32)
+        ).astype(jnp.bfloat16)
+        cp = remote(part.at[2, rr], rx.at[rr], px_s.at[n], px_r.at[n], to_x)
+        cp.start()
+        px.append(cp)
+    down_slice(3)
+    pc[1].wait_recv()
+    pz = []
+    for n, d in enumerate(steps):
+        rr = rowsof(up_to(d))
+        px[n].wait_recv()
+        sm = (
+            part[3, rr, :].astype(jnp.float32)
+            + rcore[1, rr, :].astype(jnp.float32)
+            + rx[rr, :].astype(jnp.float32)
+        )
+        if d:
+            part[3, rr, :] = sm.astype(jnp.bfloat16)
+            cp = remote(part.at[3, rr], rz.at[d - 1], pz_s.at[d], pz_r.at[d], (y, up_to(d), e))
+            cp.start()
+            pz.append(cp)
+        else:
+            res[...] = res[...] + sm
+    for cp in pz:
+        cp.wait_recv()
+    fin = res[...]
+    for d in range(1, nz):
+        fin = fin + rz[d - 1].astype(jnp.float32)
+    out_ref[...] = fin.astype(jnp.bfloat16)
+    for cp in kv + qc + mc + gz + sends + pc + px + pz:
+        cp.wait_send()
+
+
+def fused(
+    hidden_in, queries, keys, values, norm_gain, routes, gate_codes, lengths, w_gate, w_up, w_down
+):
+    nz = lax.axis_size("attn")
+    tok, width = queries.shape
+    rows, full, ffl = nz * tok, hidden_in.shape[1], w_gate.shape[2]
+    bf, f32, dma = jnp.bfloat16, jnp.float32, pltpu.SemaphoreType.DMA
+    vm = pl.BlockSpec(memory_space=pltpu.VMEM)
+    hbm = pl.BlockSpec(memory_space=pl.ANY)
+    return pl.pallas_call(
+        functools.partial(fused_kernel, nz),
+        out_shape=jax.ShapeDtypeStruct((tok, width), bf),
+        in_specs=[vm] * 6 + [pl.BlockSpec(memory_space=pltpu.SMEM)] + [hbm] * 4,
+        out_specs=vm,
+        scratch_shapes=[
+            pltpu.VMEM((SLOTS, full, CW), bf),
+            pltpu.VMEM((rows, keys.shape[1]), bf),
+            pltpu.VMEM((rows, keys.shape[1]), bf),
+            pltpu.VMEM((tok, width), bf),
+            pltpu.VMEM((tok, width), f32),
+            pltpu.VMEM((4, rows, width), bf),
+            pltpu.VMEM((rows, 128), f32),
+            pltpu.VMEM((4, tok, 128), f32),
+            pltpu.VMEM((rows, ffl), bf),
+            pltpu.VMEM((4, rows, width), bf),
+            pltpu.VMEM((2, rows, width), bf),
+            pltpu.VMEM((rows, width), bf),
+            pltpu.VMEM((nz - 1, tok, width), bf),
+            dma((SLOTS, full // ffl)),
+            dma,
+            dma((2, nz)), dma((2, nz)),
+            dma((3,)), dma((3,)),
+            dma((nz,)), dma((nz,)),
+            dma((nz,)), dma((nz,)),
+            dma((nz,)), dma((nz,)),
+            dma((2, nz)), dma((2, nz)),
+            dma((2,)), dma((2,)),
+            dma((nz,)), dma((nz,)),
+            dma((nz,)), dma((nz,)),
+        ],
+        compiler_params=pltpu.CompilerParams(
+            collective_id=0, has_side_effects=True, vmem_limit_bytes=62 * 2**20
+        ),
+    )(
+        queries, keys, values, norm_gain.reshape(1, full), routes, gate_codes, lengths,
+        hidden_in, w_gate, w_up, w_down,
+    )
+
+
+def fits(mesh, w_gate):
+    nz, ffl = mesh.shape["attn"], w_gate.shape[2] // mesh.shape["attn"]
+    return nz == 4 and mesh.shape["expert"] == 4 and 3 * ffl == w_gate.shape[1]
+
+
 def solution(mesh):
     placed = (
         P(("groups", "attn"), None),
@@ -96,10 +436,14 @@
         P("expert", None, "attn"),
         P("expert", "attn", None),
     )
-    return jax.shard_map(
-        local,
-        mesh=mesh,
-        in_specs=placed,
-        out_specs=P(("groups", "attn"), "expert"),
-        check_vma=False,
-    )
+
+    def run(*args):
+        return jax.shard_map(
+            fused if fits(mesh, args[8]) else local,
+            mesh=mesh,
+            in_specs=placed,
+            out_specs=P(("groups", "attn"), "expert"),
+            check_vma=False,
+        )(*args)
+
+    return run

time: 255 us -> 117 us (0.46)
  waiting for transfers between devices: 157 us -> 0 us
  Pallas kernels: 0 us -> 110 us
  matrix products: 38.2 us -> 0 us
  blocking collectives: 37.4 us -> 0 us
  between operations: 13.2 us -> 0.01 us
  other arithmetic: 6.62 us -> 0 us
  local copies, waits for them, and re-layouts: 2.36 us -> 5.69 us
    pallas_call x0 -> x1, Pallas kernels: none -> 110 us  [fused(): pl.pallas_call(functools.partial(fused_kernel, nz), out_shape=jax.ShapeDt...]
    all_gather x1 -> x0, waiting for transfers between devices: 63.9 us -> none  [local(): block_rows = lax.all_gather(masked, 'attn', axis=0, tiled=True)]
    reduce_scatter x1 -> x0, waiting for transfers between devices: 58.4 us -> none  [local(): lax.psum_scatter(jnp.dot(activated, down_w, preferred_element_type=jnp.fl...]
    dot_general x4 -> x0, matrix products: 37.8 us -> none  [the longest x1 23.8 us: local(): jnp.dot(activated, down_w, preferred_element_type=jnp.float32)]
    all_gather x3 -> x0, blocking collectives: 37.4 us -> none  [the longest x1 15.3 us: local(): lax.all_gather(keys, 'attn', axis=0, tiled=True)]
    psum x1 -> x0, waiting for transfers between devices: 34.8 us -> none  [local(): lax.psum(combined.astype(jnp.bfloat16), 'expert').astype(jnp.float32)]
    convert_element_type x3 -> x0, other arithmetic: 3.88 us -> none  [the longest x1 2.23 us: local(): combined.astype(jnp.bfloat16)]
    unnamed x10 -> x3, local copies, waits for them, and re-layouts: 0.63 us -> 4.36 us
  transfers between devices with their start and end apart: 3 -> 0, of which waited for: 3 -> 0; matrix products, arithmetic and copies ran while one was open for 0% -> 0% of each run, Pallas kernels for 0% -> 0%
where the time goes in v1:
time: 117 us; the launch traced here: 116 us
  Pallas kernels  110 us (94%)
  local copies, waits for them, and re-layouts  5.69 us (5%)
    pallas_call x1, Pallas kernels, fused(): pl.pallas_call(functools.partial(fused_kernel, nz), out_shape=jax.ShapeDt...  110 us
    unnamed x3, local copies, waits for them, and re-layouts  4.36 us

profile of v1, /device:TPU:0, one launch (start us, length us, event | category | flops | bytes accessed | tf_op | source)
XLA Modules:
  0.0 116.0 jit_solution(2533702977903484167)
XLA Ops:
  0.0 1.3 %reshape.3.gain_ref = bf16[1,6144]{1,0:T(2,128)(2,1)} reshape(bf16[6144]{0:T(1024)(128)(2,1)} %param.15) | data formatting | bytes 24576 | tf_op jit(solution)/shard_map/reshape | solution.py:415
  1.3 1.4 %copy.12.routes_ref = s32[64,2]{1,0:T(8,128)} copy(s32[64,2]{0,1:T(2,128)} %param.16) | data formatting | bytes 1024 | tf_op args[5]
  2.7 1.4 %copy.13.codes_ref = s32[64,2]{1,0:T(8,128)} copy(s32[64,2]{0,1:T(2,128)} %param.17) | data formatting | bytes 1024 | tf_op args[6]
  4.1 110.3 %shard_map.109 = bf16[64,1536]{1,0:T(8,128)(2,1)} custom-call(bf16[64,1536]{1,0:T(8,128)(2,1)} %q_ref.1, bf16[64,256]{1,0:T(8,128)(2,1)} %k_ref.1, bf16[64,256]{1,0:T(8,128)(2,1)} %v_ref.1, bf16[1,6144]{1,0:T(2,128)(2,1)} %reshape.3.gain_ref, s32[64,2]{1,0:T(8,128)} %copy.12.routes_ref, s32[64,2]{1,0:T(8,128)} %copy.13.codes_ref, s32[4]{0:T(128)} %len_ref.1, ...), custom_call_target="tpu_custom_call" | custom-call | tf_op jit(solution)/shard_map/pallas_call | solution.py:380
  114.4 1.6 %copy.15 = bf16[64,1536]{1,0:T(8,128)(2,1)} copy(bf16[64,1536]{1,0:T(8,128)(2,1)} %shard_map.109) | data formatting | bytes 393216

commit v2 on v1

--- a/solution.py
+++ b/solution.py
@@ -86,8 +86,8 @@
 
 
 MESH = pl.DeviceIdType.MESH
-SLOTS = 14
-CW = 256
+SLOTS = 6
+CW = 512
 
 
 def remote(src, dst, send, recv, dev):
@@ -178,11 +178,16 @@
 
     lane = lax.broadcasted_iota(jnp.int32, (tok, 128), 1)
     codes = codes_ref[...].astype(jnp.float32)
-    share = codes / (codes[:, 0:1] + codes[:, 1:2])
-    routes = routes_ref[...]
-    wts = jnp.where(routes[:, 0:1] == lane, share[:, 0:1], 0.0) + jnp.where(
-        routes[:, 1:2] == lane, share[:, 1:2], 0.0
-    )
+    csum = codes[0:1, :] + codes[1:2, :]
+    eye = lax.broadcasted_iota(jnp.int32, (tok, tok), 0) == lax.broadcasted_iota(
+        jnp.int32, (tok, tok), 1
+    )
+    wts = jnp.zeros((tok, 128), jnp.float32)
+    for x in range(4):
+        hit = jnp.where(routes_ref[...] == x, codes, 0.0)
+        row = (hit[0:1, :] + hit[1:2, :]) / csum
+        col = jnp.sum(jnp.where(eye, row, 0.0), axis=1, keepdims=True)
+        wts = wts + jnp.where(lane == x, col, 0.0)
 
     qpos = z * tok + lax.broadcasted_iota(jnp.int32, (tok, rows), 0)
     kpos = lax.broadcasted_iota(jnp.int32, (tok, rows), 1)
@@ -201,25 +206,26 @@
 
     per_group = QH // KVH
     total = jnp.zeros((tok, 1), jnp.float32)
-    for h in range(width // HD):
-        g = h // per_group
-        cols = slice(h * HD, (h + 1) * HD)
+    mask = jnp.concatenate([allowed] * per_group, axis=0)
+    for g in range(width // HD // per_group):
         gcols = slice(g * HD, (g + 1) * HD)
+        heads = [slice(h * HD, (h + 1) * HD) for h in range(g * per_group, (g + 1) * per_group)]
+        qs = jnp.concatenate([q_ref[:, c] for c in heads], axis=0)
         sc = lax.dot_general(
-            q_ref[:, cols], kall[:, gcols], (((1,), (1,)), ((), ())),
-            preferred_element_type=jnp.float32,
+            qs, kall[:, gcols], (((1,), (1,)), ((), ())), preferred_element_type=jnp.float32
         ) * (1.0 / math.sqrt(HD))
-        sc = jnp.where(allowed, sc, NEG_FILL)
+        sc = jnp.where(mask, sc, NEG_FILL)
         top = jnp.max(sc, axis=1, keepdims=True)
-        w = jnp.where(allowed, jnp.exp(sc - top), 0.0)
+        w = jnp.where(mask, jnp.exp(sc - top), 0.0)
         tot = jnp.sum(w, axis=1, keepdims=True)
         num = jnp.dot(w.astype(jnp.bfloat16), vall[:, gcols], preferred_element_type=jnp.float32)
-        att = (num / tot).astype(jnp.bfloat16)
-        r = hid[:, cols].astype(jnp.float32) + att.astype(jnp.float32)
-        res[:, cols] = r
-        total = total + jnp.sum(r * r, axis=1, keepdims=True)
-        gn = gain_ref[:, pl.ds(pl.multiple_of(e * width + h * HD, HD), HD)].astype(jnp.float32)
-        gall[e, rowsof(z), cols] = (r * gn).astype(jnp.bfloat16)
+        att = (num / tot).astype(jnp.bfloat16).astype(jnp.float32)
+        for n, cols in enumerate(heads):
+            r = hid[:, cols].astype(jnp.float32) + att[n * tok : (n + 1) * tok, :]
+            res[:, cols] = r
+            total = total + jnp.sum(r * r, axis=1, keepdims=True)
+            gn = gain_ref[:, pl.ds(pl.multiple_of(e * width + cols.start, HD), HD)].astype(jnp.float32)
+            gall[e, rowsof(z), cols] = (r * gn).astype(jnp.bfloat16)
 
     own = gall.at[e, rowsof(z)]
     sends = []
@@ -291,8 +297,8 @@
         sg = lax.rem(2 * j, SLOTS)
         su = lax.rem(2 * j + 1, SLOTS)
         gate_copy(j, sg).wait()
+        up_copy(j, su).wait()
         gate = big(sg) * scol
-        up_copy(j, su).wait()
         upv = big(su) * scol
         hv = (gate / (1.0 + jnp.exp(-gate))) * upv
         act[:, pl.ds(pl.multiple_of(j * CW, CW), CW)] = hv.astype(jnp.bfloat16)
@@ -412,7 +418,7 @@
             collective_id=0, has_side_effects=True, vmem_limit_bytes=62 * 2**20
         ),
     )(
-        queries, keys, values, norm_gain.reshape(1, full), routes, gate_codes, lengths,
+        queries, keys, values, norm_gain.reshape(1, full), routes.T, gate_codes.T, lengths,
         hidden_in, w_gate, w_up, w_down,
     )
 

time: 117 us -> 91.9 us (0.79)
  Pallas kernels: 110 us -> 88.3 us
  local copies, waits for them, and re-layouts: 5.69 us -> 2.94 us
    pallas_call x1, Pallas kernels: 110 us -> 88.3 us  [fused(): pl.pallas_call(functools.partial(fused_kernel, nz), out_shape=jax.ShapeDt...]
    unnamed x3 -> x1, local copies, waits for them, and re-layouts: 4.36 us -> 1.62 us
where the time goes in v2:
time: 91.9 us; the launch traced here: 91.2 us
  Pallas kernels  88.3 us (96%)
  local copies, waits for them, and re-layouts  2.94 us (3%)
    pallas_call x1, Pallas kernels, fused(): pl.pallas_call(functools.partial(fused_kernel, nz), out_shape=jax.ShapeDt...  88.3 us

profile of v2, /device:TPU:0, one launch (start us, length us, event | category | flops | bytes accessed | tf_op | source)
XLA Modules:
  0.0 91.2 jit_solution(8750464368147549732)
XLA Ops:
  0.0 1.3 %reshape.3.gain_ref = bf16[1,6144]{1,0:T(2,128)(2,1)} reshape(bf16[6144]{0:T(1024)(128)(2,1)} %param.15) | data formatting | bytes 24576 | tf_op jit(solution)/shard_map/reshape | solution.py:421
  1.3 88.3 %shard_map.109 = bf16[64,1536]{1,0:T(8,128)(2,1)} custom-call(bf16[64,1536]{1,0:T(8,128)(2,1)} %q_ref.1, bf16[64,256]{1,0:T(8,128)(2,1)} %k_ref.1, bf16[64,256]{1,0:T(8,128)(2,1)} %v_ref.1, bf16[1,6144]{1,0:T(2,128)(2,1)} %reshape.3.gain_ref, s32[2,64]{1,0:T(2,128)} %bitcast.2, s32[2,64]{1,0:T(2,128)} %bitcast.3, s32[4]{0:T(128)} %len_ref.1, ...), custom_call_target="tpu_custom_call" | custom-call | tf_op jit(solution)/shard_map/pallas_call | solution.py:386
  89.6 1.6 %copy.13 = bf16[64,1536]{1,0:T(8,128)(2,1)} copy(bf16[64,1536]{1,0:T(8,128)(2,1)} %shard_map.109) | data formatting | bytes 393216

commit v3 on v2

--- a/solution.py
+++ b/solution.py
@@ -99,7 +99,7 @@
 def fused_kernel(
     nz, q_ref, k_ref, v_ref, gain_ref, routes_ref, codes_ref, len_ref, hid_hbm, wg_hbm, wu_hbm, wd_hbm,
     out_ref,
-    wbuf, kall, vall, hid, res, gall, meta, ssq, act, part, rcore, rx, rz,
+    wbuf, kall, vall, hid, res, gall, meta, ssq, act, part, rcore, rx, rz, pacc,
     wsem, hsem, kv_s, kv_r, q_s, q_r, m_s, m_r, gz_s, gz_r, gx_s, gx_r, gc_s, gc_r,
     pc_s, pc_r, px_s, px_r, pz_s, pz_r,
 ):
@@ -116,7 +116,6 @@
     three = wbuf.shape[1] // ffl
     ex, ec, ed = (1 - xx) * 2 + cc, xx * 2 + 1 - cc, (1 - xx) * 2 + 1 - cc
     to_x, to_c = (y, z, ex), (y, z, ec)
-    order = [ed, ec, ex, e]
 
     def rowsof(zi):
         return pl.ds(pl.multiple_of(zi * tok, tok), tok)
@@ -139,7 +138,7 @@
 
     def down_copies(k, slot):
         pos = k // per_slice
-        ep = jnp.where(pos == 0, ed, jnp.where(pos == 1, ec, jnp.where(pos == 2, ex, e)))
+        ep = jnp.where(pos == 0, ed, jnp.where(pos == 1, ex, jnp.where(pos == 2, ec, e)))
         base = ep * width + (k % per_slice) * (three * CW)
         return [
             pltpu.make_async_copy(
@@ -264,7 +263,24 @@
     for d in range(1, nz):
         gz[d - 1].wait_recv()
         forward(down_to(d), d)
+    def half(slot, slices):
+        acc = jnp.zeros((rows, CW), jnp.float32)
+        for i in slices:
+            acc = acc + jnp.dot(
+                gall[i], wbuf[slot, pl.ds(pl.multiple_of(i * width, width), width), :],
+                preferred_element_type=jnp.float32,
+            )
+        return acc
+
     for d in range(nz):
+        blk = gall.at[ec, rowsof(down_to(d))]
+        remote(blk, blk, gc_s.at[0, d], gc_r.at[0, d], to_c).wait_recv()
+    for d in range(nz):
+        if d < SLOTS // 2:
+            gate_copy(d, 2 * d).wait()
+            up_copy(d, 2 * d + 1).wait()
+            pacc[2 * d] = half(2 * d, (e, ec))
+            pacc[2 * d + 1] = half(2 * d + 1, (e, ec))
         zi = down_to(d)
         blk = gall.at[ex, rowsof(zi)]
         remote(blk, blk, gx_s.at[d], gx_r.at[d], to_x).wait_recv()
@@ -275,31 +291,24 @@
         cp.wait_recv()
     for d in range(nz):
         zi = down_to(d)
-        for i, pe in enumerate((ec, ed)):
-            blk = gall.at[pe, rowsof(zi)]
-            remote(blk, blk, gc_s.at[i, d], gc_r.at[i, d], to_c).wait_recv()
+        blk = gall.at[ed, rowsof(zi)]
+        remote(blk, blk, gc_s.at[1, d], gc_r.at[1, d], to_c).wait_recv()
 
     scol = meta[:, 4:5]
     mlane = lax.broadcasted_iota(jnp.int32, (rows, 128), 1)
     wcol = jnp.sum(jnp.where(mlane == e, meta[...], 0.0), axis=1, keepdims=True)
 
-    def big(slot):
-        acc = jnp.zeros((rows, CW), jnp.float32)
-        for i in range(4):
-            acc = acc + jnp.dot(
-                gall[i], wbuf[slot, i * width : (i + 1) * width, :],
-                preferred_element_type=jnp.float32,
-            )
-        return acc
-
-    @pl.loop(0, n_pair)
-    def _(j):
+    def pair(j, early):
         sg = lax.rem(2 * j, SLOTS)
         su = lax.rem(2 * j + 1, SLOTS)
-        gate_copy(j, sg).wait()
-        up_copy(j, su).wait()
-        gate = big(sg) * scol
-        upv = big(su) * scol
+        if early:
+            gate = (pacc[2 * j] + half(sg, (ex, ed))) * scol
+            upv = (pacc[2 * j + 1] + half(su, (ex, ed))) * scol
+        else:
+            gate_copy(j, sg).wait()
+            up_copy(j, su).wait()
+            gate = half(sg, (e, ec, ex, ed)) * scol
+            upv = half(su, (e, ec, ex, ed)) * scol
         hv = (gate / (1.0 + jnp.exp(-gate))) * upv
         act[:, pl.ds(pl.multiple_of(j * CW, CW), CW)] = hv.astype(jnp.bfloat16)
         nxt = 2 * j + SLOTS
@@ -313,6 +322,14 @@
         def _():
             for cp in down_copies(nxt - 2 * n_pair, sg) + down_copies(nxt + 1 - 2 * n_pair, su):
                 cp.start()
+
+    @pl.loop(0, SLOTS // 2)
+    def _(j):
+        pair(j, True)
+
+    @pl.loop(SLOTS // 2, n_pair)
+    def _(j):
+        pair(j, False)
 
     def down_slice(pos):
         @pl.loop(0, per_slice)
@@ -328,24 +345,27 @@
                 col = pl.ds(pl.multiple_of((i * three + t) * CW, CW), CW)
                 part[pos, :, col] = (o * wcol).astype(jnp.bfloat16)
 
-    pc = []
-    for pos in range(2):
-        down_slice(pos)
-        cp = remote(part.at[pos], rcore.at[pos], pc_s.at[pos], pc_r.at[pos], to_c)
+    def to_core(pos):
+        cp = remote(part.at[pos], rcore.at[pos // 2], pc_s.at[pos // 2], pc_r.at[pos // 2], to_c)
         cp.start()
-        pc.append(cp)
-    down_slice(2)
+        return cp
+
+    down_slice(0)
+    pc = [to_core(0)]
+    down_slice(1)
     pc[0].wait_recv()
     steps = [2, 1, 3, 0] if nz == 4 else list(range(1, nz)) + [0]
     px = []
     for n, d in enumerate(steps):
         rr = rowsof(up_to(d))
-        part[2, rr, :] = (
-            part[2, rr, :].astype(jnp.float32) + rcore[0, rr, :].astype(jnp.float32)
+        part[1, rr, :] = (
+            part[1, rr, :].astype(jnp.float32) + rcore[0, rr, :].astype(jnp.float32)
         ).astype(jnp.bfloat16)
-        cp = remote(part.at[2, rr], rx.at[rr], px_s.at[n], px_r.at[n], to_x)
+        cp = remote(part.at[1, rr], rx.at[rr], px_s.at[n], px_r.at[n], to_x)
         cp.start()
         px.append(cp)
+    down_slice(2)
+    pc.append(to_core(2))
     down_slice(3)
     pc[1].wait_recv()
     pz = []
@@ -402,6 +422,7 @@
             pltpu.VMEM((2, rows, width), bf),
             pltpu.VMEM((rows, width), bf),
             pltpu.VMEM((nz - 1, tok, width), bf),
+            pltpu.VMEM((SLOTS, rows, CW), f32),
             dma((SLOTS, full // ffl)),
             dma,
             dma((2, nz)), dma((2, nz)),

time: 91.9 us -> 86.9 us (0.946)
  Pallas kernels: 88.3 us -> 83.7 us
    pallas_call x1, Pallas kernels: 88.3 us -> 83.7 us  [fused(): pl.pallas_call(functools.partial(fused_kernel, nz), out_shape=jax.ShapeDt...]
where the time goes in v3:
time: 86.9 us; the launch traced here: 86.7 us
  Pallas kernels  83.7 us (96%)
  local copies, waits for them, and re-layouts  2.94 us (3%)
    pallas_call x1, Pallas kernels, fused(): pl.pallas_call(functools.partial(fused_kernel, nz), out_shape=jax.ShapeDt...  83.7 us

profile of v3, /device:TPU:0, one launch (start us, length us, event | category | flops | bytes accessed | tf_op | source)
XLA Modules:
  0.0 86.7 jit_solution(258276066710709344)
XLA Ops:
  0.0 1.3 %reshape.3.gain_ref = bf16[1,6144]{1,0:T(2,128)(2,1)} reshape(bf16[6144]{0:T(1024)(128)(2,1)} %param.15) | data formatting | bytes 24576 | tf_op jit(solution)/shard_map/reshape | solution.py:442
  1.3 83.7 %shard_map.109 = bf16[64,1536]{1,0:T(8,128)(2,1)} custom-call(bf16[64,1536]{1,0:T(8,128)(2,1)} %q_ref.1, bf16[64,256]{1,0:T(8,128)(2,1)} %k_ref.1, bf16[64,256]{1,0:T(8,128)(2,1)} %v_ref.1, bf16[1,6144]{1,0:T(2,128)(2,1)} %reshape.3.gain_ref, s32[2,64]{1,0:T(2,128)} %bitcast.2, s32[2,64]{1,0:T(2,128)} %bitcast.3, s32[4]{0:T(128)} %len_ref.1, ...), custom_call_target="tpu_custom_call" | custom-call | tf_op jit(solution)/shard_map/pallas_call | solution.py:406
  85.1 1.6 %copy.13 = bf16[64,1536]{1,0:T(8,128)(2,1)} copy(bf16[64,1536]{1,0:T(8,128)(2,1)} %shard_map.109) | data formatting | bytes 393216
